TPU v7x, 256 devices: a whole 4x4x8 slice. The times are simulated.
256 devices in a mesh: cand: 64 (over y, z, x_lo), param: 4 (over x_hi, core).
Axes of the slice: x: 4 (x_hi: 2, x_lo: 2; x = x_hi * 2 + x_lo), y: 4, z: 8, core: 2. Of those that a mesh axis runs over, the one named last changes fastest.
Arguments:
- candidate_rows: bfloat16 [32768, 8192], P('cand', 'param'), may hold values from -6 to 6
- sigma_rows: bfloat16 [32768, 8192], P('cand', 'param'), may hold values from -0.0625 to 0.0625
- sigma_sq_rows: bfloat16 [32768, 8192], P('cand', 'param'), may hold values from -0.0625 to 0.0625
- direction: bfloat16 [32768], P('cand'), may hold values from -0.119628906 to 0.119628906
- relaxed: float32 [32768], P(('cand', 'param')), may hold values from 0.05 to 0.95
Outputs:
- newton_residual: float32 [32768], P(('cand', 'param'))
All inputs are finite; a program needn't handle non-finite values.
Results may differ from a plain program's by a relative error of at most 0.0003.
Values may be sent and summed in bfloat16 or wider, within the bound.
A program may use at most 64 MiB of HBM per device.

v0:
```python
import jax
import jax.numpy as jnp
from jax import lax
from jax.sharding import PartitionSpec as P

PARTNERS = 2


barrier_weight = 0.1


def shortened(value):

    def short(part):
        return part.astype(jnp.bfloat16) if part.dtype == jnp.float32 else part

    return jax.tree.map(short, value)


def shifted(value, axis, by):
    peers = lax.axis_size(axis)
    return lax.ppermute(value, axis, [(i, (i + by) % peers) for i in range(peers)])


def gram_tile(left_one, left_two, right_one, right_two):
    width = left_one.shape[0]
    dims = (((1,), (1,)), ((), ()))
    prod_one = lax.dot_general(left_one, right_one, dims, preferred_element_type=jnp.float32)
    prod_two = lax.dot_general(left_two, right_two, dims, preferred_element_type=jnp.float32)
    summed = lax.psum_scatter(
        jnp.concatenate([prod_one, prod_two], axis=1), "param", scatter_dimension=0, tiled=True
    )
    return (2.0 * summed[:, :width] * summed[:, width:], summed[:, width:])


def apply_rows(tile, vector):
    return jnp.dot(tile, vector, precision=lax.Precision.HIGHEST)


def advance(moving):
    return jax.tree.map(
        lambda part, own: part.astype(own.dtype), shifted(shortened(moving), "cand", 1), moving
    )


def body(candidate_rows, sigma_rows, sigma_sq_rows, direction, relaxed):
    width = candidate_rows.shape[0]
    share = width // lax.axis_size("param")
    first_row = lax.axis_index("param") * share
    own_vec = direction.astype(jnp.float32)
    own_slice = lax.dynamic_slice_in_dim(own_vec, first_row, share, 0)
    diag_tile, second_gram = gram_tile(candidate_rows, candidate_rows, sigma_rows, sigma_sq_rows)
    residual_output = apply_rows(diag_tile, own_vec)
    square = lax.dynamic_slice_in_dim(second_gram, first_row, share, 1)
    diag_terms = jnp.diagonal(square)
    moving = (sigma_rows, sigma_sq_rows, direction)
    backward = (candidate_rows, direction)
    for step in range(1, PARTNERS + 1):
        moving = advance(moving)
        backward = shifted((backward[0], backward[1]), "cand", -1)
        tile_before, unused_one = gram_tile(candidate_rows, candidate_rows, moving[0], moving[1])
        residual_output = residual_output + apply_rows(tile_before, moving[2].astype(jnp.float32))
        tile_after, unused_two = gram_tile(sigma_rows, sigma_sq_rows, backward[0], backward[0])
        residual_output = residual_output + apply_rows(tile_after, backward[1].astype(jnp.float32))
    grad = -diag_terms - barrier_weight * (1.0 / relaxed - 1.0 / (1.0 - relaxed))
    curve = barrier_weight * (1.0 / (relaxed * relaxed) + 1.0 / ((1.0 - relaxed) * (1.0 - relaxed)))
    return residual_output + grad + curve * own_slice


def solution(mesh):
    return jax.shard_map(
        body,
        mesh=mesh,
        in_specs=(
            P("cand", "param"),
            P("cand", "param"),
            P("cand", "param"),
            P("cand"),
            P(("cand", "param")),
        ),
        out_specs=P(("cand", "param")),
        check_vma=False,
    )
```

profile of v0, /device:TPU:5, one launch (start us, length us, event | category | flops | bytes accessed | tf_op | source)
XLA Modules:
  0.0 399.8 jit_solution(5514837042274218412)
XLA Ops:
  6.5 3.6 fusion.19
  10.2 1.4 fusion.20
  11.6 1.5 pad_maximum_fusion
  13.1 0.0 reduce-scatter.10.cloned.1.call-start
  13.2 8.7 %collective-permute-start.3 = (bf16[512,2048]{1,0:T(8,128)(2,1)}, bf16[512,2048]{1,0:T(8,128)(2,1)S(1)}, u32[]{:S(2)}, u32[]{:S(2)}) collective-permute-start(bf16[512,2048]{1,0:T(8,128)(2,1)} %param.5), channel_id=1, source_target_pairs={{0,252},{4,0},{8,4},{12,8},{16,12},{20,16},{24,20},{28,24},{32,28}... | collective-permute-start | bytes 6291464 | tf_op jit(solution)/shard_map/ppermute | solution.py:22
  21.9 49.4 %collective-permute-done.3 = bf16[512,2048]{1,0:T(8,128)(2,1)S(1)} collective-permute-done((bf16[512,2048]{1,0:T(8,128)(2,1)}, bf16[512,2048]{1,0:T(8,128)(2,1)S(1)}, u32[]{:S(2)}, u32[]{:S(2)}) %collective-permute-start.3) | collective-permute-done | bytes 2097184 | tf_op jit(solution)/shard_map/ppermute | solution.py:22
  71.3 1.3 fusion.24
  72.6 0.1 copy-done.9
  72.7 1.3 fusion.23
  74.0 1.5 pad_maximum_fusion.2
  75.5 0.0 reduce-scatter.8.cloned.1.call-start
  75.5 0.1 collective-permute-start
  75.6 2.8 collective-permute-start.1
  78.4 52.5 %collective-permute-done = bf16[512,2048]{1,0:T(8,128)(2,1)S(1)} collective-permute-done((bf16[512,2048]{1,0:T(8,128)(2,1)}, bf16[512,2048]{1,0:T(8,128)(2,1)S(1)}, u32[]{:S(2)}, u32[]{:S(2)}) %collective-permute-start) | collective-permute-done | bytes 2097184 | tf_op jit(solution)/shard_map/ppermute | solution.py:22
  130.9 3.7 fusion.21
  134.6 41.2 %collective-permute-done.1 = bf16[512,2048]{1,0:T(8,128)(2,1)S(1)} collective-permute-done((bf16[512,2048]{1,0:T(8,128)(2,1)S(1)}, bf16[512,2048]{1,0:T(8,128)(2,1)S(1)}, u32[]{:S(2)}, u32[]{:S(2)}) %collective-permute-start.1) | collective-permute-done | bytes 2097184 | tf_op jit(solution)/shard_map/ppermute | solution.py:22
  175.8 1.3 fusion.22
  177.1 0.1 copy-done.7
  177.2 1.5 pad_maximum_fusion.1
  178.7 0.0 reduce-scatter.14.cloned.1.call-start
  178.8 10.3 %collective-permute-start.8 = (bf16[512,2048]{1,0:T(8,128)(2,1)}, bf16[512,2048]{1,0:T(8,128)(2,1)S(1)}, u32[]{:S(2)}, u32[]{:S(2)}) collective-permute-start(bf16[512,2048]{1,0:T(8,128)(2,1)} %copy-done.9), channel_id=1, source_target_pairs={{0,252},{4,0},{8,4},{12,8},{16,12},{20,16},{24,20},{28,24},{32,28}... | collective-permute-start | bytes 6291464 | tf_op jit(solution)/shard_map/ppermute | solution.py:22
  189.1 44.4 %collective-permute-done.8 = bf16[512,2048]{1,0:T(8,128)(2,1)S(1)} collective-permute-done((bf16[512,2048]{1,0:T(8,128)(2,1)}, bf16[512,2048]{1,0:T(8,128)(2,1)S(1)}, u32[]{:S(2)}, u32[]{:S(2)}) %collective-permute-start.8) | collective-permute-done | bytes 2097184 | tf_op jit(solution)/shard_map/ppermute | solution.py:22
  233.4 1.3 fusion.28
  234.7 1.3 fusion.27
  236.0 1.5 pad_maximum_fusion.4
  237.6 0.0 reduce-scatter.12.cloned.1.call-start
  237.6 0.1 collective-permute-start.5
  237.7 3.1 collective-permute-start.6
  240.9 49.6 %collective-permute-done.5 = bf16[512,2048]{1,0:T(8,128)(2,1)S(1)} collective-permute-done((bf16[512,2048]{1,0:T(8,128)(2,1)}, bf16[512,2048]{1,0:T(8,128)(2,1)S(1)}, u32[]{:S(2)}, u32[]{:S(2)}) %collective-permute-start.5) | collective-permute-done | bytes 2097184 | tf_op jit(solution)/shard_map/ppermute | solution.py:22
  290.4 1.3 fusion.25
  291.7 43.6 %collective-permute-done.6 = bf16[512,2048]{1,0:T(8,128)(2,1)S(1)} collective-permute-done((bf16[512,2048]{1,0:T(8,128)(2,1)}, bf16[512,2048]{1,0:T(8,128)(2,1)S(1)}, u32[]{:S(2)}, u32[]{:S(2)}) %collective-permute-start.6) | collective-permute-done | bytes 2097184 | tf_op jit(solution)/shard_map/ppermute | solution.py:22
  335.4 1.3 fusion.26
  336.7 1.6 pad_maximum_fusion.3
  338.3 0.7 copy-done
  338.9 1.7 collective-permute-start.2
  340.6 11.9 %collective-permute-start.4 = (bf16[512]{0:T(512)(128)(2,1)S(1)}, bf16[512]{0:T(512)(128)(2,1)S(1)}, u32[]{:S(2)}, u32[]{:S(2)}) collective-permute-start(bf16[512]{0:T(512)(128)(2,1)S(1)} %copy-done), channel_id=1, source_target_pairs={{0,252},{4,0},{8,4},{12,8},{16,12},{20,16},{24,20},{28,24},{32,28}... | collective-permute-start | bytes 3080 | tf_op jit(solution)/shard_map/ppermute | solution.py:22
  352.5 1.0 collective-permute-done.2
  353.5 5.7 %collective-permute-start.9 = (bf16[512]{0:T(512)(128)(2,1)S(1)}, bf16[512]{0:T(512)(128)(2,1)S(1)}, u32[]{:S(2)}, u32[]{:S(2)}) collective-permute-start(bf16[512]{0:T(512)(128)(2,1)S(1)} %collective-permute-done.4), channel_id=1, source_target_pairs={{0,252},{4,0},{8,4},{12,8},{16,12},{20,16},{24,20},{28,24},{32,28}... | collective-permute-start | bytes 3080 | tf_op jit(solution)/shard_map/ppermute | solution.py:22
  359.2 0.9 collective-permute-done.7
  360.1 0.0 reduce-scatter.6.cloned.1.call-done
  360.2 1.0 slice.44
  361.1 1.3 gather_fusion
  362.4 1.3 convolution_bitcast_fusion.4
  363.7 1.3 convolution_bitcast_fusion.2
  365.1 1.3 fusion.1
  366.3 1.3 convolution_bitcast_fusion
  367.6 23.9 %reduce-scatter.12.cloned.1.call-done = f32[128,1024]{0,1:T(8,128)} async-done(((f32[512,1024]{0,1:T(8,128)}), f32[128,1024]{0,1:T(8,128)}) %reduce-scatter.12.cloned.1.call-update) | async-done | bytes 524304 | tf_op jit(solution)/shard_map/reduce_scatter | solution.py:30
  391.5 1.8 fusion.5
  (39 shorter events, 0.2 us)
Async XLA Ops:
  6.5 3.7 copy-start.1
  6.5 353.6 %reduce-scatter.6.cloned.1.call-start = ((), (), s32[]{:S(2)}) async-start(), calls=%async_computation.5 | async-start | bytes 2621440 | tf_op jit(solution)/shard_map/reduce_scatter | solution.py:30
  6.5 3.7 copy-start.4
  13.1 350.6 %reduce-scatter.10.cloned.1.call-start = ((), (), s32[]{:S(2)}) async-start(), calls=%async_computation.7 | async-start | bytes 2621440 | tf_op jit(solution)/shard_map/reduce_scatter | solution.py:30
  13.2 59.5 %copy-start.2 = (bf16[512,2048]{1,0:T(8,128)(2,1)S(1)}, bf16[512,2048]{1,0:T(8,128)(2,1)}, u32[]{:S(2)}) copy-start(bf16[512,2048]{1,0:T(8,128)(2,1)} %param.6) | copy-start | bytes 6291460
  13.2 58.1 %collective-permute-start.3 = (bf16[512,2048]{1,0:T(8,128)(2,1)}, bf16[512,2048]{1,0:T(8,128)(2,1)S(1)}, u32[]{:S(2)}, u32[]{:S(2)}) collective-permute-start(bf16[512,2048]{1,0:T(8,128)(2,1)} %param.5), channel_id=1, source_target_pairs={{0,252},{4,0},{8,4},{12,8},{16,12},{20,16},{24,20},{28,24},{32,28}... | collective-permute-start | bytes 6291464 | tf_op jit(solution)/shard_map/ppermute | solution.py:22
  71.3 1.4 copy-start.9
  75.5 289.6 %reduce-scatter.8.cloned.1.call-start = ((), (), s32[]{:S(2)}) async-start(), calls=%async_computation.6 | async-start | bytes 2621440 | tf_op jit(solution)/shard_map/reduce_scatter | solution.py:30
  75.5 100.2 %copy-start.5 = (bf16[512,2048]{1,0:T(8,128)(2,1)S(1)}, bf16[512,2048]{1,0:T(8,128)(2,1)}, u32[]{:S(2)}) copy-start(bf16[512,2048]{1,0:T(8,128)(2,1)} %param.5) | copy-start | bytes 6291460
  75.5 55.4 %collective-permute-start = (bf16[512,2048]{1,0:T(8,128)(2,1)}, bf16[512,2048]{1,0:T(8,128)(2,1)S(1)}, u32[]{:S(2)}, u32[]{:S(2)}) collective-permute-start(bf16[512,2048]{1,0:T(8,128)(2,1)} %param.6), channel_id=1, source_target_pairs={{0,4},{4,8},{8,12},{12,16},{16,20},{20,24},{24,28},{28,32},{32,36}... | collective-permute-start | bytes 6291464 | tf_op jit(solution)/shard_map/ppermute | solution.py:22
  75.6 100.1 %collective-permute-start.1 = (bf16[512,2048]{1,0:T(8,128)(2,1)S(1)}, bf16[512,2048]{1,0:T(8,128)(2,1)S(1)}, u32[]{:S(2)}, u32[]{:S(2)}) collective-permute-start(bf16[512,2048]{1,0:T(8,128)(2,1)S(1)} %copy-done.1), channel_id=1, source_target_pairs={{0,4},{4,8},{8,12},{12,16},{16,20},{20,24},{24,28},{28,32},{32,36}... | collective-permute-start | bytes 6291464 | tf_op jit(solution)/shard_map/ppermute | solution.py:22
  130.9 3.7 copy-start.8
  175.8 1.4 copy-start.7
  178.7 187.6 %reduce-scatter.14.cloned.1.call-start = ((), (), s32[]{:S(2)}) async-start(), calls=%async_computation.9 | async-start | bytes 2621440 | tf_op jit(solution)/shard_map/reduce_scatter | solution.py:30
  178.8 56.0 %copy-start.3 = (bf16[512,2048]{1,0:T(8,128)(2,1)S(1)}, bf16[512,2048]{1,0:T(8,128)(2,1)}, u32[]{:S(2)}) copy-start(bf16[512,2048]{1,0:T(8,128)(2,1)} %param.6) | copy-start | bytes 6291460
  178.8 54.7 %collective-permute-start.8 = (bf16[512,2048]{1,0:T(8,128)(2,1)}, bf16[512,2048]{1,0:T(8,128)(2,1)S(1)}, u32[]{:S(2)}, u32[]{:S(2)}) collective-permute-start(bf16[512,2048]{1,0:T(8,128)(2,1)} %copy-done.9), channel_id=1, source_target_pairs={{0,252},{4,0},{8,4},{12,8},{16,12},{20,16},{24,20},{28,24},{32,28}... | collective-permute-start | bytes 6291464 | tf_op jit(solution)/shard_map/ppermute | solution.py:22
  237.6 52.9 %copy-start.6 = (bf16[512,2048]{1,0:T(8,128)(2,1)S(1)}, bf16[512,2048]{1,0:T(8,128)(2,1)}, u32[]{:S(2)}) copy-start(bf16[512,2048]{1,0:T(8,128)(2,1)} %param.5) | copy-start | bytes 6291460
  237.6 153.9 %reduce-scatter.12.cloned.1.call-start = ((), (), s32[]{:S(2)}) async-start(), calls=%async_computation.8 | async-start | bytes 2621440 | tf_op jit(solution)/shard_map/reduce_scatter | solution.py:30
  237.6 52.8 %collective-permute-start.5 = (bf16[512,2048]{1,0:T(8,128)(2,1)}, bf16[512,2048]{1,0:T(8,128)(2,1)S(1)}, u32[]{:S(2)}, u32[]{:S(2)}) collective-permute-start(bf16[512,2048]{1,0:T(8,128)(2,1)} %copy-done.8), channel_id=1, source_target_pairs={{0,4},{4,8},{8,12},{12,16},{16,20},{20,24},{24,28},{28,32},{32,36}... | collective-permute-start | bytes 6291464 | tf_op jit(solution)/shard_map/ppermute | solution.py:22
  237.7 97.7 %collective-permute-start.6 = (bf16[512,2048]{1,0:T(8,128)(2,1)}, bf16[512,2048]{1,0:T(8,128)(2,1)S(1)}, u32[]{:S(2)}, u32[]{:S(2)}) collective-permute-start(bf16[512,2048]{1,0:T(8,128)(2,1)} %copy-done.7), channel_id=1, source_target_pairs={{0,4},{4,8},{8,12},{12,16},{16,20},{20,24},{24,28},{28,32},{32,36}... | collective-permute-start | bytes 6291464 | tf_op jit(solution)/shard_map/ppermute | solution.py:22
  338.2 0.7 copy-start
  338.2 53.2 %copy-start.10 = (f32[128]{0:T(128)S(1)}, f32[128]{0:T(128)}, u32[]{:S(2)}) copy-start(f32[128]{0:T(128)} %param.9) | copy-start | bytes 1540
  338.9 14.6 %collective-permute-start.2 = (bf16[512]{0:T(512)(128)(2,1)S(1)}, bf16[512]{0:T(512)(128)(2,1)S(1)}, u32[]{:S(2)}, u32[]{:S(2)}) collective-permute-start(bf16[512]{0:T(512)(128)(2,1)S(1)} %copy-done), channel_id=1, source_target_pairs={{0,4},{4,8},{8,12},{12,16},{16,20},{20,24},{24,28},{28,32},{32,36}... | collective-permute-start | bytes 3080 | tf_op jit(solution)/shard_map/ppermute | solution.py:22
  340.6 12.9 %collective-permute-start.4 = (bf16[512]{0:T(512)(128)(2,1)S(1)}, bf16[512]{0:T(512)(128)(2,1)S(1)}, u32[]{:S(2)}, u32[]{:S(2)}) collective-permute-start(bf16[512]{0:T(512)(128)(2,1)S(1)} %copy-done), channel_id=1, source_target_pairs={{0,252},{4,0},{8,4},{12,8},{16,12},{20,16},{24,20},{28,24},{32,28}... | collective-permute-start | bytes 3080 | tf_op jit(solution)/shard_map/ppermute | solution.py:22
  353.5 6.6 %collective-permute-start.7 = (bf16[512]{0:T(512)(128)(2,1)S(1)}, bf16[512]{0:T(512)(128)(2,1)S(1)}, u32[]{:S(2)}, u32[]{:S(2)}) collective-permute-start(bf16[512]{0:T(512)(128)(2,1)S(1)} %collective-permute-done.2), channel_id=1, source_target_pairs={{0,4},{4,8},{8,12},{12,16},{16,20},{20,24},{24,28},{28,32},{32,36}... | collective-permute-start | bytes 3080 | tf_op jit(solution)/shard_map/ppermute | solution.py:22
  353.5 6.6 %collective-permute-start.9 = (bf16[512]{0:T(512)(128)(2,1)S(1)}, bf16[512]{0:T(512)(128)(2,1)S(1)}, u32[]{:S(2)}, u32[]{:S(2)}) collective-permute-start(bf16[512]{0:T(512)(128)(2,1)S(1)} %collective-permute-done.4), channel_id=1, source_target_pairs={{0,252},{4,0},{8,4},{12,8},{16,12},{20,16},{24,20},{28,24},{32,28}... | collective-permute-start | bytes 3080 | tf_op jit(solution)/shard_map/ppermute | solution.py:22
Sparse Core Ops, SparseCore 0:
  13.2 61.0 reduce-scatter.5
  77.3 54.9 reduce-scatter.9
  178.8 60.7 reduce-scatter.7
  242.5 57.2 reduce-scatter.13
  338.4 53.0 reduce-scatter.11
where the time goes:
time: 404 us; the launch traced here: 400 us
  waiting for transfers between devices  307 us (76%)
  starting transfers between devices  44.6 us (11%)
  matrix products  24.5 us (6%)
  between operations  13.4 us (3%)
  other arithmetic  7.62 us (2%)
    ppermute x10, waiting for transfers between devices, shifted(): lax.ppermute(value, axis, [(i, (i + by) % peers) for i in range(peers)])  282 us
    ppermute x10, starting transfers between devices, shifted(): lax.ppermute(value, axis, [(i, (i + by) % peers) for i in range(peers)])  44.4 us
    reduce_scatter x5, waiting for transfers between devices, gram_tile(): lax.psum_scatter(jnp.concatenate([prod_one, prod_two], axis=1), 'param',...  23.9 us
    dot_general x5, matrix products, gram_tile(): lax.dot_general(left_one, right_one, dims, preferred_element_type=jnp.flo...  11.1 us
  transfers between devices with their start and end apart: 15, of which 9 were waited for; matrix products, arithmetic and copies ran while one was open for 7% of the time, Pallas kernels for 0%

commit v1 on v0

v1 whole, which is shorter than its diff:
```python
import jax
import jax.numpy as jnp
from jax import lax
from jax.experimental import pallas as pl
from jax.experimental.pallas import tpu as pltpu
from jax.sharding import PartitionSpec as P

PARTNERS = 2
barrier_weight = 0.1

MESH = pl.DeviceIdType.MESH
ROWS = 128
CHUNKS = 4
STEPS = 3 * CHUNKS
HALF = 256
LAST = (((1,), (1,)), ((), ()))
FIRST = (((1,), (0,)), ((), ()))


def exact_dot(left, right, dims):
    return lax.dot_general(
        left, right, dims, precision=lax.Precision.HIGHEST, preferred_element_type=jnp.float32
    )


def kernel(
    a_in, s_in, q_in, v_in, out,
    rows, sq, vec, g_send, g_recv, g_own, k_send, k_recv, col, m_send, m_recv,
    load_sem, z_send_sem, z_recv_sem, x_send_sem, x_recv_sem, g_send_sem, g_recv_sem,
    k_send_sem, k_recv_sem, m_send_sem, m_recv_sem, v_send_sem, v_recv_sem,
):
    cand, param = lax.axis_index("cand"), lax.axis_index("param")
    blocks = lax.axis_size("cand")
    odd, core, x_hi = lax.rem(cand, 2), lax.rem(param, 2), param // 2

    def block_at(by):
        return lax.rem(cand + blocks + by, blocks)

    loads = []
    for chunk in range(CHUNKS):
        loads.append((a_in.at[pl.ds(chunk * ROWS, ROWS)], rows.at[0, chunk]))
    for half in range(2):
        part = pl.ds(half * HALF, HALF)
        loads.append((s_in.at[part], sq.at[half, pl.ds(0, HALF)]))
        loads.append((q_in.at[part], sq.at[half, pl.ds(HALF, HALF)]))
    loads = [
        pltpu.make_async_copy(source, target, load_sem.at[i])
        for i, (source, target) in enumerate(loads)
    ]
    for load in loads:
        load.start()

    barrier = pltpu.get_barrier_semaphore()
    partners = 0
    for by in (-2, -1, 0, 1, 2):
        for turn in range(4):
            if by == 0 and turn == 0:
                continue
            pl.semaphore_signal(
                barrier, inc=1, device_id=(block_at(by), lax.rem(param + turn, 4)),
                device_id_type=MESH,
            )
            partners += 1
    pl.semaphore_wait(barrier, partners)

    def to_two_before(chunk):
        return pltpu.make_async_remote_copy(
            src_ref=a_in.at[pl.ds(chunk * ROWS, ROWS)], dst_ref=rows.at[2, chunk],
            send_sem=z_send_sem.at[chunk], recv_sem=z_recv_sem.at[chunk],
            device_id=(block_at(-2), param), device_id_type=MESH,
        )

    def to_pair(chunk, source):
        return pltpu.make_async_remote_copy(
            src_ref=source, dst_ref=rows.at[1, chunk],
            send_sem=x_send_sem.at[chunk], recv_sem=x_recv_sem.at[chunk],
            device_id=(cand + 1 - 2 * odd, param), device_id_type=MESH,
        )

    def vec_to(by):
        return pltpu.make_async_remote_copy(
            src_ref=v_in, dst_ref=vec.at[by - 1],
            send_sem=v_send_sem.at[by - 1], recv_sem=v_recv_sem.at[by - 1],
            device_id=(block_at(-by), param), device_id_type=MESH,
        )

    for chunk in range(CHUNKS):
        to_two_before(chunk).start()

        @pl.when(odd == 1)
        def _():
            to_pair(chunk, a_in.at[pl.ds(chunk * ROWS, ROWS)]).start()

    for by in (1, 2):
        vec_to(by).start()

    col[...] = jnp.zeros_like(col)
    for load in loads:
        load.wait()

    def place(step):
        late = step - CHUNKS
        own = step < CHUNKS
        chunk = jnp.where(own, step, late // 2)
        by = jnp.where(own, 0, 2 - lax.rem(late + 2 * CHUNKS, 2))
        return by, chunk

    def to_core(step):
        return pltpu.make_async_remote_copy(
            src_ref=g_send.at[step], dst_ref=g_recv.at[step],
            send_sem=g_send_sem.at[step], recv_sem=g_recv_sem.at[step],
            device_id=(cand, param + 1 - 2 * core), device_id_type=MESH,
        )

    def to_chip(step):
        return pltpu.make_async_remote_copy(
            src_ref=k_send.at[step], dst_ref=k_recv.at[step],
            send_sem=k_send_sem.at[step], recv_sem=k_recv_sem.at[step],
            device_id=(cand, lax.rem(param + 2, 4)), device_id_type=MESH,
        )

    def message(index, slot, by, target):
        return pltpu.make_async_remote_copy(
            src_ref=m_send.at[index], dst_ref=m_recv.at[slot],
            send_sem=m_send_sem.at[index], recv_sem=m_recv_sem.at[slot],
            device_id=(block_at(by), target), device_id_type=MESH,
        )

    def products(step):
        by, chunk = place(step)

        @pl.when(by == 1)
        def _():
            to_pair(chunk, rows.at[2, chunk]).wait_recv()

        @pl.when(by == 2)
        def _():
            to_two_before(chunk).wait_recv()

            @pl.when(odd == 0)
            def _():
                to_pair(chunk, rows.at[2, chunk]).start()

        g_send[step] = lax.dot_general(
            rows[by, chunk], sq[1 - core], LAST, preferred_element_type=jnp.float32
        )
        to_core(step).start()
        g_own[step] = lax.dot_general(
            rows[by, chunk], sq[core], LAST, preferred_element_type=jnp.float32
        )

    def between_cores(step):
        to_core(step).wait_recv()
        total = g_own[step] + g_recv[step]
        g_own[step] = total
        k_send[step] = total[:, HALF:]
        to_chip(step).start()

    def between_chips(step):
        by, chunk = place(step)
        to_chip(step).wait_recv()
        total = g_own[step]
        tile = total[:, :HALF] * (total[:, HALF:] + k_recv[step])
        own_vec = 2.0 * jnp.concatenate([v_in[2 * core], v_in[2 * core + 1]], axis=1)
        m_send[step] = exact_dot(own_vec, tile, LAST)

        @pl.when(by > 0)
        def _():
            col[...] += exact_dot(2.0 * vec[by - 1, chunk], tile, FIRST)

        @pl.when(jnp.logical_and(by == 0, chunk // 2 == core))
        def _():
            square = jnp.where(
                lax.rem(chunk, 2) == 0, total[:, HALF : HALF + ROWS], total[:, HALF + ROWS :]
            )
            line = lax.broadcasted_iota(jnp.int32, (ROWS, ROWS), 0)
            place_in = lax.broadcasted_iota(jnp.int32, (ROWS, ROWS), 1)
            square = jnp.where(line == place_in, square, 0.0)
            m_send[step] -= jnp.broadcast_to(jnp.sum(square, axis=0, keepdims=True), (8, ROWS))

        stays = jnp.logical_and(by == 0, chunk == param)

        @pl.when(stays)
        def _():
            m_recv[param] = m_send[step]

        @pl.when(jnp.logical_not(stays))
        def _():
            message(step, by * 4 + param, by, chunk).start()

    def one(step, carry):
        @pl.when(jnp.logical_and(step >= 1, step <= STEPS))
        def _():
            between_cores(step - 1)

        @pl.when(step < STEPS)
        def _():
            products(step)

        @pl.when(step >= LAG)
        def _():
            between_chips(step - LAG)

        return carry

    LAG = 3
    lax.fori_loop(0, CHUNKS, one, 0)
    for by in (1, 2):
        vec_to(by).wait()
    lax.fori_loop(CHUNKS, STEPS + LAG, one, 0)

    for part in range(2):
        m_send[STEPS + part] = col[:, part * ROWS : (part + 1) * ROWS]
        target = 2 * core + part

        @pl.when(target == param)
        def _():
            m_recv[12 + x_hi] = m_send[STEPS + part]

        @pl.when(target != param)
        def _():
            message(STEPS + part, 12 + x_hi, 0, target).start()

    for source in range(4):
        @pl.when(source != param)
        def _():
            message(0, source, 0, param).wait_recv()

        message(0, 4 + source, 1, param).wait_recv()
        message(0, 8 + source, 2, param).wait_recv()
    for high in range(2):
        @pl.when(2 * high + param // 2 != param)
        def _():
            message(0, 12 + high, 0, param).wait_recv()

    out[...] = jnp.sum(m_recv[...], axis=0)

    def drain(step, carry):
        to_core(step).wait_send()
        to_chip(step).wait_send()
        by, chunk = place(step)

        @pl.when(jnp.logical_not(jnp.logical_and(by == 0, chunk == param)))
        def _():
            message(step, 0, by, chunk).wait_send()

        return carry

    lax.fori_loop(0, STEPS, drain, 0)
    for part in range(2):
        @pl.when(2 * core + part != param)
        def _():
            message(STEPS + part, 0, 0, param).wait_send()

    for chunk in range(CHUNKS):
        to_two_before(chunk).wait_send()
        to_pair(chunk, rows.at[2, chunk]).wait_send()


def hessian_product(candidate_rows, sigma_rows, sigma_sq_rows, vectors):
    width, depth = candidate_rows.shape
    f32 = jnp.float32
    dma = pltpu.SemaphoreType.DMA
    return pl.pallas_call(
        kernel,
        out_shape=jax.ShapeDtypeStruct((8, ROWS), f32),
        in_specs=[pl.BlockSpec(memory_space=pl.ANY)] * 3 + [pl.BlockSpec(memory_space=pltpu.VMEM)],
        out_specs=pl.BlockSpec(memory_space=pltpu.VMEM),
        scratch_shapes=[
            pltpu.VMEM((3, CHUNKS, ROWS, depth), jnp.bfloat16),
            pltpu.VMEM((2, width, depth), jnp.bfloat16),
            pltpu.VMEM((2, CHUNKS, 8, ROWS), f32),
            pltpu.VMEM((STEPS, ROWS, width), f32),
            pltpu.VMEM((STEPS, ROWS, width), f32),
            pltpu.VMEM((STEPS, ROWS, width), f32),
            pltpu.VMEM((STEPS, ROWS, HALF), f32),
            pltpu.VMEM((STEPS, ROWS, HALF), f32),
            pltpu.VMEM((8, HALF), f32),
            pltpu.VMEM((STEPS + 2, 8, ROWS), f32),
            pltpu.VMEM((14, 8, ROWS), f32),
            dma((CHUNKS + 4,)),
            dma((CHUNKS,)), dma((CHUNKS,)), dma((CHUNKS,)), dma((CHUNKS,)),
            dma((STEPS,)), dma((STEPS,)), dma((STEPS,)), dma((STEPS,)),
            dma((STEPS + 2,)), dma((14,)), dma((2,)), dma((2,)),
        ],
        compiler_params=pltpu.CompilerParams(
            collective_id=1, has_side_effects=True, vmem_limit_bytes=40 * 2**20
        ),
        name="hessian_product",
    )(candidate_rows, sigma_rows, sigma_sq_rows, vectors)


def body(candidate_rows, sigma_rows, sigma_sq_rows, direction, relaxed):
    width = candidate_rows.shape[0]
    share = width // lax.axis_size("param")
    first_row = lax.axis_index("param") * share
    own_vec = direction.astype(jnp.float32)
    own_slice = lax.dynamic_slice_in_dim(own_vec, first_row, share, 0)
    vectors = jnp.broadcast_to(own_vec.reshape(CHUNKS, 1, ROWS), (CHUNKS, 8, ROWS))
    product = hessian_product(candidate_rows, sigma_rows, sigma_sq_rows, vectors)[0]
    slope = barrier_weight * (1.0 / relaxed - 1.0 / (1.0 - relaxed))
    curve = barrier_weight * (1.0 / (relaxed * relaxed) + 1.0 / ((1.0 - relaxed) * (1.0 - relaxed)))
    return product - slope + curve * own_slice


def solution(mesh):
    return jax.shard_map(
        body,
        mesh=mesh,
        in_specs=(
            P("cand", "param"),
            P("cand", "param"),
            P("cand", "param"),
            P("cand"),
            P(("cand", "param")),
        ),
        out_specs=P(("cand", "param")),
        check_vma=False,
    )
```

time: 404 us -> 148 us (0.37)
  waiting for transfers between devices: 307 us -> 0 us
  Pallas kernels: 0 us -> 142 us
  starting transfers between devices: 44.6 us -> 0 us
  matrix products: 24.5 us -> 0 us
  between operations: 13.4 us -> 0.02 us
  other arithmetic: 7.62 us -> 1.27 us
    ppermute x10 -> x0, waiting for transfers between devices: 282 us -> none  [shifted(): lax.ppermute(value, axis, [(i, (i + by) % peers) for i in range(peers)])]
    pallas_call x0 -> x1, Pallas kernels: none -> 142 us  [hessian_product(): pl.pallas_call(kernel, out_shape=jax.ShapeDtypeStruct((8, ROWS), f32), in...]
    ppermute x10 -> x0, starting transfers between devices: 44.4 us -> none  [shifted(): lax.ppermute(value, axis, [(i, (i + by) % peers) for i in range(peers)])]
    dot_general x15 -> x0, matrix products: 24.5 us -> none  [the longest x5 11.1 us: gram_tile(): lax.dot_general(left_one, right_one, dims, preferred_element_type=jnp.flo...]
    reduce_scatter x5 -> x0, waiting for transfers between devices: 23.9 us -> none  [gram_tile(): lax.psum_scatter(jnp.concatenate([prod_one, prod_two], axis=1), 'param',...]
    concatenate x6 -> x0, other arithmetic: 7.61 us -> none  [the longest x5 7.61 us: gram_tile(): jnp.concatenate([prod_one, prod_two], axis=1)]
  transfers between devices with their start and end apart: 15 -> 0, of which waited for: 9 -> 0; matrix products, arithmetic and copies ran while one was open for 7% -> 0% of each run, Pallas kernels for 0% -> 0%
where the time goes in v1:
time: 148 us
  Pallas kernels  142 us (96%)
  local copies, waits for them, and re-layouts  4.78 us (3%)
    pallas_call x1, Pallas kernels, hessian_product(): pl.pallas_call(kernel, out_shape=jax.ShapeDtypeStruct((8, ROWS), f32), in...  142 us
    unnamed x8, local copies, waits for them, and re-layouts  4.78 us

profile of v1, /device:TPU:5, one launch (start us, length us, event | category | flops | bytes accessed | tf_op | source)
XLA Modules:
  0.0 147.8 jit_solution(12906391659230396187)
XLA Ops:
  0.0 0.7 convert_bitcast_fusion
  0.7 0.0 copy-start
  0.7 1.6 %copy-done = bf16[512,2048]{1,0:T(8,128)(2,1)S(1)} copy-done((bf16[512,2048]{1,0:T(8,128)(2,1)S(1)}, bf16[512,2048]{1,0:T(8,128)(2,1)}, u32[]{:S(2)}) %copy-start) | copy-done | bytes 2097176
  2.3 0.0 copy-start.1
  2.3 1.6 %copy-done.1 = bf16[512,2048]{1,0:T(8,128)(2,1)S(1)} copy-done((bf16[512,2048]{1,0:T(8,128)(2,1)S(1)}, bf16[512,2048]{1,0:T(8,128)(2,1)}, u32[]{:S(2)}) %copy-start.1) | copy-done | bytes 2097176
  3.9 0.0 copy-start.2
  3.9 1.6 %copy-done.2 = bf16[512,2048]{1,0:T(8,128)(2,1)S(1)} copy-done((bf16[512,2048]{1,0:T(8,128)(2,1)S(1)}, bf16[512,2048]{1,0:T(8,128)(2,1)}, u32[]{:S(2)}) %copy-start.2) | copy-done | bytes 2097176
  5.5 0.0 copy-start.3
  5.5 141.7 %hessian_product.1 = f32[8,128]{1,0:T(8,128)S(1)} custom-call(bf16[512,2048]{1,0:T(8,128)(2,1)S(1)} %copy-done, bf16[512,2048]{1,0:T(8,128)(2,1)S(1)} %copy-done.1, bf16[512,2048]{1,0:T(8,128)(2,1)S(1)} %copy-done.2, f32[4,8,128]{2,1,0:T(8,128)S(1)} %broadcast_in_dim.8.v_in), custom_call_target="tpu_custom_call" | custom-call | tf_op jit(solution)/shard_map/hessian_product/pallas_call | solution.py:264
  147.2 0.0 copy-done.3
  147.2 0.6 fusion
  (1 shorter events, 0.0 us)
Async XLA Ops:
  0.7 1.6 %copy-start = (bf16[512,2048]{1,0:T(8,128)(2,1)S(1)}, bf16[512,2048]{1,0:T(8,128)(2,1)}, u32[]{:S(2)}) copy-start(bf16[512,2048]{1,0:T(8,128)(2,1)} %a_in.1) | copy-start | bytes 6291460
  2.3 1.6 %copy-start.1 = (bf16[512,2048]{1,0:T(8,128)(2,1)S(1)}, bf16[512,2048]{1,0:T(8,128)(2,1)}, u32[]{:S(2)}) copy-start(bf16[512,2048]{1,0:T(8,128)(2,1)} %s_in.1) | copy-start | bytes 6291460
  3.9 1.6 %copy-start.2 = (bf16[512,2048]{1,0:T(8,128)(2,1)S(1)}, bf16[512,2048]{1,0:T(8,128)(2,1)}, u32[]{:S(2)}) copy-start(bf16[512,2048]{1,0:T(8,128)(2,1)} %q_in.1) | copy-start | bytes 6291460
  5.5 141.7 %copy-start.3 = (f32[128]{0:T(128)S(1)}, f32[128]{0:T(128)}, u32[]{:S(2)}) copy-start(f32[128]{0:T(128)} %param.9) | copy-start | bytes 1540

commit v2 on v1

--- a/solution.py
+++ b/solution.py
@@ -9,10 +9,15 @@
 barrier_weight = 0.1
 
 MESH = pl.DeviceIdType.MESH
-ROWS = 128
-CHUNKS = 4
+ROWS = 64
+CHUNKS = 8
 STEPS = 3 * CHUNKS
 HALF = 256
+SHARE = 128
+SPAN = 256
+AHEAD = 2
+LAG = 4
+REACH = 125.0
 LAST = (((1,), (1,)), ((), ()))
 FIRST = (((1,), (0,)), ((), ()))
 
@@ -25,7 +30,7 @@
 
 def kernel(
     a_in, s_in, q_in, v_in, out,
-    rows, sq, vec, g_send, g_recv, g_own, k_send, k_recv, col, m_send, m_recv,
+    rows, sq, sqt, vec, g_send, g_recv, g_own, k_send, k_recv, col, line, m_send, m_recv,
     load_sem, z_send_sem, z_recv_sem, x_send_sem, x_recv_sem, g_send_sem, g_recv_sem,
     k_send_sem, k_recv_sem, m_send_sem, m_recv_sem, v_send_sem, v_recv_sem,
 ):
@@ -63,9 +68,12 @@
             partners += 1
     pl.semaphore_wait(barrier, partners)
 
+    def own_rows(chunk):
+        return a_in.at[pl.ds(pl.multiple_of(chunk * ROWS, ROWS), ROWS)]
+
     def to_two_before(chunk):
         return pltpu.make_async_remote_copy(
-            src_ref=a_in.at[pl.ds(chunk * ROWS, ROWS)], dst_ref=rows.at[2, chunk],
+            src_ref=own_rows(chunk), dst_ref=rows.at[2, chunk],
             send_sem=z_send_sem.at[chunk], recv_sem=z_recv_sem.at[chunk],
             device_id=(block_at(-2), param), device_id_type=MESH,
         )
@@ -84,26 +92,37 @@
             device_id=(block_at(-by), param), device_id_type=MESH,
         )
 
-    for chunk in range(CHUNKS):
+    def send_own(chunk):
         to_two_before(chunk).start()
 
         @pl.when(odd == 1)
         def _():
-            to_pair(chunk, a_in.at[pl.ds(chunk * ROWS, ROWS)]).start()
-
+            to_pair(chunk, own_rows(chunk)).start()
+
+    send_own(0)
     for by in (1, 2):
         vec_to(by).start()
 
     col[...] = jnp.zeros_like(col)
-    for load in loads:
+    for load in loads[CHUNKS:]:
         load.wait()
 
+    def turn(piece, carry):
+        at = pl.ds(pl.multiple_of(piece * SPAN, SPAN), SPAN)
+        for half in range(2):
+            sqt[half, at, :] = sq[half, :, at].T
+        return carry
+
+    lax.fori_loop(0, sq.shape[2] // SPAN, turn, 0)
+    for load in loads[:CHUNKS]:
+        load.wait()
+
     def place(step):
-        late = step - CHUNKS
-        own = step < CHUNKS
-        chunk = jnp.where(own, step, late // 2)
-        by = jnp.where(own, 0, 2 - lax.rem(late + 2 * CHUNKS, 2))
-        return by, chunk
+        late = jnp.maximum(step - CHUNKS, 0)
+        far = jnp.logical_or(late == 0, jnp.logical_and(lax.rem(late, 2) == 1, late < 2 * CHUNKS - 1))
+        by = jnp.where(step < CHUNKS, 0, jnp.where(far, 2, 1))
+        chunk = jnp.where(far, (late + 1) // 2, jnp.maximum(late - 1, 0) // 2)
+        return by, jnp.where(step < CHUNKS, step, chunk)
 
     def to_core(step):
         return pltpu.make_async_remote_copy(
@@ -141,85 +160,115 @@
             def _():
                 to_pair(chunk, rows.at[2, chunk]).start()
 
+            @pl.when(chunk + AHEAD < CHUNKS)
+            def _():
+                send_own(chunk + AHEAD)
+
+        for early in range(1, AHEAD):
+            @pl.when(step == 3 * early)
+            def _():
+                send_own(early)
+
         g_send[step] = lax.dot_general(
-            rows[by, chunk], sq[1 - core], LAST, preferred_element_type=jnp.float32
+            rows[by, chunk], sqt[1 - core], FIRST, preferred_element_type=jnp.float32
         )
         to_core(step).start()
         g_own[step] = lax.dot_general(
-            rows[by, chunk], sq[core], LAST, preferred_element_type=jnp.float32
-        )
+            rows[by, chunk], sqt[core], FIRST, preferred_element_type=jnp.float32
+        )
+
+    def coded(values):
+        scale = jnp.max(jnp.abs(values), axis=0, keepdims=True) * 1.01 + 1e-30
+        scale = scale.astype(jnp.bfloat16).astype(jnp.float32)
+        power = jnp.exp2(jnp.abs(values) * (2.0 * REACH / scale) - REACH)
+        return jnp.where(values < 0.0, -power, power), scale
+
+    def decoded(code, scale):
+        size = (jnp.log2(jnp.abs(code)) + REACH) * (scale * (0.5 / REACH))
+        return jnp.where(code < 0.0, -size, size)
 
     def between_cores(step):
         to_core(step).wait_recv()
         total = g_own[step] + g_recv[step]
         g_own[step] = total
-        k_send[step] = total[:, HALF:]
+        code, scale = coded(total[:, HALF:])
+        k_send[step, :ROWS] = code.astype(jnp.bfloat16)
+        k_send[step, ROWS:] = jnp.broadcast_to(scale, (16, HALF)).astype(jnp.bfloat16)
         to_chip(step).start()
 
     def between_chips(step):
         by, chunk = place(step)
         to_chip(step).wait_recv()
         total = g_own[step]
-        tile = total[:, :HALF] * (total[:, HALF:] + k_recv[step])
+        other = decoded(
+            k_recv[step, :ROWS].astype(jnp.float32),
+            k_recv[step, ROWS:].astype(jnp.float32)[:1],
+        )
+        tile = total[:, :HALF] * (total[:, HALF:] + other)
         own_vec = 2.0 * jnp.concatenate([v_in[2 * core], v_in[2 * core + 1]], axis=1)
-        m_send[step] = exact_dot(own_vec, tile, LAST)
+        line[by, lax.rem(chunk, 2)] = exact_dot(own_vec, tile, LAST)
 
         @pl.when(by > 0)
         def _():
-            col[...] += exact_dot(2.0 * vec[by - 1, chunk], tile, FIRST)
-
-        @pl.when(jnp.logical_and(by == 0, chunk // 2 == core))
-        def _():
-            square = jnp.where(
-                lax.rem(chunk, 2) == 0, total[:, HALF : HALF + ROWS], total[:, HALF + ROWS :]
-            )
-            line = lax.broadcasted_iota(jnp.int32, (ROWS, ROWS), 0)
-            place_in = lax.broadcasted_iota(jnp.int32, (ROWS, ROWS), 1)
-            square = jnp.where(line == place_in, square, 0.0)
-            m_send[step] -= jnp.broadcast_to(jnp.sum(square, axis=0, keepdims=True), (8, ROWS))
-
-        stays = jnp.logical_and(by == 0, chunk == param)
-
-        @pl.when(stays)
-        def _():
-            m_recv[param] = m_send[step]
-
-        @pl.when(jnp.logical_not(stays))
-        def _():
-            message(step, by * 4 + param, by, chunk).start()
+            pair = vec[jnp.maximum(by - 1, 0), chunk // 2]
+            part = jnp.where(lax.rem(chunk, 2) == 0, pair[:, :ROWS], pair[:, ROWS:])
+            col[...] += exact_dot(2.0 * part, tile, FIRST)
+
+        @pl.when(jnp.logical_and(by == 0, chunk // 4 == core))
+        def _():
+            down = lax.broadcasted_iota(jnp.int32, (ROWS, HALF), 0)
+            across = lax.broadcasted_iota(jnp.int32, (ROWS, HALF), 1)
+            square = jnp.where(down + lax.rem(chunk, 4) * ROWS == across, total[:, HALF:], 0.0)
+            col[...] -= jnp.broadcast_to(jnp.sum(square, axis=0, keepdims=True), (8, HALF))
+
+        target = chunk // 2
+        index = by * 4 + target
+        stays = jnp.logical_and(by == 0, target == param)
+        whole = lax.rem(chunk, 2) == 1
+
+        @pl.when(whole)
+        def _():
+            m_send[index] = jnp.concatenate([line[by, 0], line[by, 1]], axis=1)
+
+        @pl.when(jnp.logical_and(whole, stays))
+        def _():
+            m_recv[param] = m_send[index]
+
+        @pl.when(jnp.logical_and(whole, jnp.logical_not(stays)))
+        def _():
+            message(index, by * 4 + param, by, target).start()
 
     def one(step, carry):
         @pl.when(jnp.logical_and(step >= 1, step <= STEPS))
         def _():
             between_cores(step - 1)
 
+        @pl.when(step >= LAG)
+        def _():
+            between_chips(step - LAG)
+
         @pl.when(step < STEPS)
         def _():
             products(step)
 
-        @pl.when(step >= LAG)
-        def _():
-            between_chips(step - LAG)
-
         return carry
 
-    LAG = 3
     lax.fori_loop(0, CHUNKS, one, 0)
     for by in (1, 2):
         vec_to(by).wait()
     lax.fori_loop(CHUNKS, STEPS + LAG, one, 0)
 
     for part in range(2):
-        m_send[STEPS + part] = col[:, part * ROWS : (part + 1) * ROWS]
+        m_send[12 + part] = col[:, part * SHARE : (part + 1) * SHARE]
         target = 2 * core + part
 
         @pl.when(target == param)
         def _():
-            m_recv[12 + x_hi] = m_send[STEPS + part]
+            m_recv[12 + x_hi] = m_send[12 + part]
 
         @pl.when(target != param)
         def _():
-            message(STEPS + part, 12 + x_hi, 0, target).start()
+            message(12 + part, 12 + x_hi, 0, target).start()
 
     for source in range(4):
         @pl.when(source != param)
@@ -238,19 +287,20 @@
     def drain(step, carry):
         to_core(step).wait_send()
         to_chip(step).wait_send()
-        by, chunk = place(step)
-
-        @pl.when(jnp.logical_not(jnp.logical_and(by == 0, chunk == param)))
-        def _():
-            message(step, 0, by, chunk).wait_send()
-
         return carry
 
     lax.fori_loop(0, STEPS, drain, 0)
+    for target in range(4):
+        @pl.when(target != param)
+        def _():
+            message(target, 0, 0, target).wait_send()
+
+        message(4 + target, 0, 1, target).wait_send()
+        message(8 + target, 0, 2, target).wait_send()
     for part in range(2):
         @pl.when(2 * core + part != param)
         def _():
-            message(STEPS + part, 0, 0, param).wait_send()
+            message(12 + part, 0, 0, param).wait_send()
 
     for chunk in range(CHUNKS):
         to_two_before(chunk).wait_send()
@@ -263,28 +313,30 @@
     dma = pltpu.SemaphoreType.DMA
     return pl.pallas_call(
         kernel,
-        out_shape=jax.ShapeDtypeStruct((8, ROWS), f32),
+        out_shape=jax.ShapeDtypeStruct((8, SHARE), f32),
         in_specs=[pl.BlockSpec(memory_space=pl.ANY)] * 3 + [pl.BlockSpec(memory_space=pltpu.VMEM)],
         out_specs=pl.BlockSpec(memory_space=pltpu.VMEM),
         scratch_shapes=[
             pltpu.VMEM((3, CHUNKS, ROWS, depth), jnp.bfloat16),
             pltpu.VMEM((2, width, depth), jnp.bfloat16),
-            pltpu.VMEM((2, CHUNKS, 8, ROWS), f32),
+            pltpu.VMEM((2, depth, width), jnp.bfloat16),
+            pltpu.VMEM((2, 4, 8, SHARE), f32),
             pltpu.VMEM((STEPS, ROWS, width), f32),
             pltpu.VMEM((STEPS, ROWS, width), f32),
             pltpu.VMEM((STEPS, ROWS, width), f32),
-            pltpu.VMEM((STEPS, ROWS, HALF), f32),
-            pltpu.VMEM((STEPS, ROWS, HALF), f32),
+            pltpu.VMEM((STEPS, ROWS + 16, HALF), jnp.bfloat16),
+            pltpu.VMEM((STEPS, ROWS + 16, HALF), jnp.bfloat16),
             pltpu.VMEM((8, HALF), f32),
-            pltpu.VMEM((STEPS + 2, 8, ROWS), f32),
-            pltpu.VMEM((14, 8, ROWS), f32),
+            pltpu.VMEM((3, 2, 8, ROWS), f32),
+            pltpu.VMEM((14, 8, SHARE), f32),
+            pltpu.VMEM((14, 8, SHARE), f32),
             dma((CHUNKS + 4,)),
             dma((CHUNKS,)), dma((CHUNKS,)), dma((CHUNKS,)), dma((CHUNKS,)),
             dma((STEPS,)), dma((STEPS,)), dma((STEPS,)), dma((STEPS,)),
-            dma((STEPS + 2,)), dma((14,)), dma((2,)), dma((2,)),
+            dma((14,)), dma((14,)), dma((2,)), dma((2,)),
         ],
         compiler_params=pltpu.CompilerParams(
-            collective_id=1, has_side_effects=True, vmem_limit_bytes=40 * 2**20
+            collective_id=1, has_side_effects=True, vmem_limit_bytes=62 * 2**20
         ),
         name="hessian_product",
     )(candidate_rows, sigma_rows, sigma_sq_rows, vectors)
@@ -296,7 +348,7 @@
     first_row = lax.axis_index("param") * share
     own_vec = direction.astype(jnp.float32)
     own_slice = lax.dynamic_slice_in_dim(own_vec, first_row, share, 0)
-    vectors = jnp.broadcast_to(own_vec.reshape(CHUNKS, 1, ROWS), (CHUNKS, 8, ROWS))
+    vectors = jnp.broadcast_to(own_vec.reshape(4, 1, SHARE), (4, 8, SHARE))
     product = hessian_product(candidate_rows, sigma_rows, sigma_sq_rows, vectors)[0]
     slope = barrier_weight * (1.0 / relaxed - 1.0 / (1.0 - relaxed))
     curve = barrier_weight * (1.0 / (relaxed * relaxed) + 1.0 / ((1.0 - relaxed) * (1.0 - relaxed)))

time: 148 us -> 101 us (0.68)
  Pallas kernels: 142 us -> 97.9 us
  local copies, waits for them, and re-layouts: 4.78 us -> 0.61 us
    pallas_call x1, Pallas kernels: 142 us -> 97.9 us  [hessian_product(): pl.pallas_call(kernel, out_shape=jax.ShapeDtypeStruct((8, SHARE), f32), i...]
    unnamed x8 -> x2, local copies, waits for them, and re-layouts: 4.78 us -> 0.01 us
where the time goes in v2:
time: 101 us
  Pallas kernels  97.9 us (97%)
  other arithmetic  1.95 us (2%)
    pallas_call x1, Pallas kernels, hessian_product(): pl.pallas_call(kernel, out_shape=jax.ShapeDtypeStruct((8, SHARE), f32), i...  97.9 us

profile of v2, /device:TPU:5, one launch (start us, length us, event | category | flops | bytes accessed | tf_op | source)
XLA Modules:
  0.0 100.5 jit_solution(13452493295381522104)
XLA Ops:
  0.0 0.7 convert_bitcast_fusion
  0.7 0.6 broadcast_in_dim.8.v_in
  1.3 0.0 copy-start
  1.3 97.9 %hessian_product.1 = f32[8,128]{1,0:T(8,128)} custom-call(bf16[512,2048]{1,0:T(8,128)(2,1)} %a_in.1, bf16[512,2048]{1,0:T(8,128)(2,1)} %s_in.1, bf16[512,2048]{1,0:T(8,128)(2,1)} %q_in.1, f32[4,8,128]{2,1,0:T(8,128)} %broadcast_in_dim.8.v_in), custom_call_target="tpu_custom_call" | custom-call | tf_op jit(solution)/shard_map/hessian_product/pallas_call | solution.py:314
  99.2 0.0 copy-done
  99.2 1.3 %fusion = f32[128]{0:T(128)} fusion(f32[512]{0:T(512)S(1)} %get-tuple-element.6, s32[]{:T(128)S(6)} %select_n.3, f32[128]{0:T(128)S(1)} %copy-done, f32[8,128]{1,0:T(8,128)} %hessian_product.1), kind=kLoop, calls=%fused_computation.3 | loop fusion | flops 1792 | bytes 2052 | tf_op jit(solution)/shard_map/add | solution.py:355
Async XLA Ops:
  1.3 97.9 %copy-start = (f32[128]{0:T(128)S(1)}, f32[128]{0:T(128)}, u32[]{:S(2)}) copy-start(f32[128]{0:T(128)} %param.9) | copy-start | bytes 1540

commit v3 on v1

v3 whole, which is shorter than its diff:
```python
import jax
import jax.numpy as jnp
from jax import lax
from jax.experimental import pallas as pl
from jax.experimental.pallas import tpu as pltpu
from jax.sharding import PartitionSpec as P

PARTNERS = 2
barrier_weight = 0.1

MESH = pl.DeviceIdType.MESH
ROWS = 128
CHUNKS = 4
STEPS = 3 * CHUNKS
PIECE = 64
PIECES = 8
HALF = 256
SPAN = 256
AHEAD = 2
LAG = 4
REACH = 125.0
LAST = (((1,), (1,)), ((), ()))
FIRST = (((1,), (0,)), ((), ()))


def exact_dot(left, right, dims):
    return lax.dot_general(
        left, right, dims, precision=lax.Precision.HIGHEST, preferred_element_type=jnp.float32
    )


def coded(values):
    scale = jnp.max(jnp.abs(values), axis=0, keepdims=True) + 1e-30
    power = jnp.exp2(jnp.abs(values) * (2.0 * REACH / scale) - REACH)
    return jnp.where(values < 0.0, -power, power), scale


def decoded(code, scale):
    size = (jnp.log2(jnp.abs(code)) + REACH) * (scale * (0.5 / REACH))
    return jnp.where(code < 0.0, -size, size)


def kernel(
    a_in, s_in, q_in, v_in, z_in, out,
    rows, sq, sqt, own_vec, vec, g_send, g_recv, g_own, k_send, k_recv, w_send, w_recv, col, m_send, m_recv,
    load_sem, z_send_sem, z_recv_sem, x_send_sem, x_recv_sem, g_send_sem, g_recv_sem,
    k_send_sem, k_recv_sem, w_send_sem, w_recv_sem, m_send_sem, m_recv_sem, v_send_sem, v_recv_sem,
):
    cand, param = lax.axis_index("cand"), lax.axis_index("param")
    blocks = lax.axis_size("cand")
    odd, core, x_hi = lax.rem(cand, 2), lax.rem(param, 2), param // 2

    def block_at(by):
        return lax.rem(cand + blocks + by, blocks)

    loads = []
    for half in range(2):
        part = pl.ds(half * HALF, HALF)
        loads.append((s_in.at[part], sq.at[half, pl.ds(0, HALF)]))
        loads.append((q_in.at[part], sq.at[half, pl.ds(HALF, HALF)]))
    loads.append((a_in, rows.at[0]))
    loads = [
        pltpu.make_async_copy(source, target, load_sem.at[i])
        for i, (source, target) in enumerate(loads)
    ]
    for load in loads:
        load.start()

    barrier = pltpu.get_barrier_semaphore()
    partners = 0
    for by in (-2, -1, 0, 1, 2):
        for turn in range(4):
            if by == 0 and turn == 0:
                continue
            pl.semaphore_signal(
                barrier, inc=1, device_id=(block_at(by), lax.rem(param + turn, 4)),
                device_id_type=MESH,
            )
            partners += 1
    for part in range(4):
        own_vec[part] = jnp.broadcast_to(v_in[part : part + 1, :].astype(jnp.float32), (8, ROWS))
    col[...] = jnp.zeros_like(col)
    pl.semaphore_wait(barrier, partners)

    def own_piece(piece):
        return a_in.at[pl.ds(pl.multiple_of(piece * PIECE, PIECE), PIECE)]

    def landing(by, piece):
        return rows.at[by, pl.ds(pl.multiple_of(piece * PIECE, PIECE), PIECE)]

    def to_two_before(piece):
        return pltpu.make_async_remote_copy(
            src_ref=own_piece(piece), dst_ref=landing(2, piece),
            send_sem=z_send_sem.at[piece], recv_sem=z_recv_sem.at[piece],
            device_id=(block_at(-2), param), device_id_type=MESH,
        )

    def to_pair(piece, source):
        return pltpu.make_async_remote_copy(
            src_ref=source, dst_ref=landing(1, piece),
            send_sem=x_send_sem.at[piece], recv_sem=x_recv_sem.at[piece],
            device_id=(cand + 1 - 2 * odd, param), device_id_type=MESH,
        )

    def vec_to(by):
        return pltpu.make_async_remote_copy(
            src_ref=own_vec, dst_ref=vec.at[by - 1],
            send_sem=v_send_sem.at[by - 1], recv_sem=v_recv_sem.at[by - 1],
            device_id=(block_at(-by), param), device_id_type=MESH,
        )

    def send_own(piece):
        to_two_before(piece).start()

        @pl.when(odd == 1)
        def _():
            to_pair(piece, own_piece(piece)).start()

    def pass_on(piece):
        to_two_before(piece).wait_recv()

        @pl.when(odd == 0)
        def _():
            to_pair(piece, landing(2, piece)).start()

        @pl.when(piece + AHEAD < PIECES)
        def _():
            send_own(piece + AHEAD)

    send_own(0)
    for by in (1, 2):
        vec_to(by).start()

    for load in loads[:4]:
        load.wait()

    def turn(piece, carry):
        at = pl.ds(pl.multiple_of(piece * SPAN, SPAN), SPAN)
        for half in range(2):
            sqt[half, at, :] = sq[half, :, at].T
        return carry

    lax.fori_loop(0, sq.shape[2] // SPAN, turn, 0)
    loads[4].wait()

    def place(step):
        late = jnp.maximum(step - CHUNKS, 0)
        by = jnp.where(step < CHUNKS, 0, 2 - lax.rem(late, 2))
        return by, jnp.where(step < CHUNKS, step, late // 2)

    def to_core(step):
        return pltpu.make_async_remote_copy(
            src_ref=g_send.at[step], dst_ref=g_recv.at[step],
            send_sem=g_send_sem.at[step], recv_sem=g_recv_sem.at[step],
            device_id=(cand, param + 1 - 2 * core), device_id_type=MESH,
        )

    def to_chip(step):
        return pltpu.make_async_remote_copy(
            src_ref=k_send.at[step], dst_ref=k_recv.at[step],
            send_sem=k_send_sem.at[step], recv_sem=k_recv_sem.at[step],
            device_id=(cand, lax.rem(param + 2, 4)), device_id_type=MESH,
        )

    def scale_to_chip(step):
        return pltpu.make_async_remote_copy(
            src_ref=w_send.at[step], dst_ref=w_recv.at[step],
            send_sem=w_send_sem.at[step], recv_sem=w_recv_sem.at[step],
            device_id=(cand, lax.rem(param + 2, 4)), device_id_type=MESH,
        )

    def message(index, slot, by, target):
        return pltpu.make_async_remote_copy(
            src_ref=m_send.at[index], dst_ref=m_recv.at[slot],
            send_sem=m_send_sem.at[index], recv_sem=m_recv_sem.at[slot],
            device_id=(block_at(by), target), device_id_type=MESH,
        )

    def products(step):
        by, chunk = place(step)

        for early in range(1, AHEAD):
            @pl.when(step == early)
            def _():
                send_own(early)

        @pl.when(step == CHUNKS)
        def _():
            pass_on(0)

        @pl.when(jnp.logical_and(step >= CHUNKS, step < STEPS - 1))
        def _():
            pass_on(step - CHUNKS + 1)

        @pl.when(by == 1)
        def _():
            for part in range(2):
                to_pair(2 * chunk + part, landing(2, 2 * chunk + part)).wait_recv()

        left = rows[by, pl.ds(pl.multiple_of(chunk * ROWS, ROWS), ROWS), :]
        g_send[step] = lax.dot_general(
            left, sqt[1 - core], FIRST, preferred_element_type=jnp.float32
        )
        to_core(step).start()
        g_own[step] = lax.dot_general(
            left, sqt[core], FIRST, preferred_element_type=jnp.float32
        )

    def between_cores(step):
        to_core(step).wait_recv()
        total = g_own[step] + g_recv[step]
        g_own[step] = total
        code, scale = coded(total[:, HALF:])
        k_send[step] = code.astype(jnp.bfloat16)
        w_send[step] = scale
        to_chip(step).start()
        scale_to_chip(step).start()

    def between_chips(step):
        by, chunk = place(step)
        to_chip(step).wait_recv()
        total = g_own[step]
        scale_to_chip(step).wait_recv()
        other = decoded(k_recv[step].astype(jnp.float32), w_recv[step])
        tile = total[:, :HALF] * (total[:, HALF:] + other)
        half_vec = jnp.concatenate([own_vec[2 * core], own_vec[2 * core + 1]], axis=1)
        m_send[step] = exact_dot(2.0 * half_vec, tile, LAST)
        stays = jnp.logical_and(by == 0, chunk == param)

        @pl.when(stays)
        def _():
            m_recv[param] = m_send[step]

        @pl.when(jnp.logical_not(stays))
        def _():
            message(step, by * 4 + param, by, chunk).start()

        @pl.when(by > 0)
        def _():
            col[...] += exact_dot(2.0 * vec[jnp.maximum(by - 1, 0), chunk], tile, FIRST)

        @pl.when(jnp.logical_and(by == 0, chunk // 2 == core))
        def _():
            down = lax.broadcasted_iota(jnp.int32, (ROWS, HALF), 0)
            across = lax.broadcasted_iota(jnp.int32, (ROWS, HALF), 1)
            square = jnp.where(down + lax.rem(chunk, 2) * ROWS == across, total[:, HALF:], 0.0)
            col[...] -= jnp.broadcast_to(jnp.sum(square, axis=0, keepdims=True), (8, HALF))

    def first(step, carry):
        products(step)

        @pl.when(step >= 1)
        def _():
            between_cores(step - 1)

        return carry

    def later(step, carry):
        products(step)

        @pl.when(step >= LAG)
        def _():
            between_chips(step - LAG)

        between_cores(step)
        return carry

    def last(step, carry):
        between_chips(step)
        return carry

    lax.fori_loop(0, CHUNKS, first, 0)
    between_cores(CHUNKS - 1)
    for by in (1, 2):
        vec_to(by).wait()
    lax.fori_loop(CHUNKS, STEPS, later, 0)
    lax.fori_loop(STEPS - LAG, STEPS, last, 0)

    for part in range(2):
        m_send[STEPS + part] = col[:, part * ROWS : (part + 1) * ROWS]
        target = 2 * core + part

        @pl.when(target == param)
        def _():
            m_recv[12 + x_hi] = m_send[STEPS + part]

        @pl.when(target != param)
        def _():
            message(STEPS + part, 12 + x_hi, 0, target).start()

    zval = z_in[...]
    slope = barrier_weight * (1.0 / zval - 1.0 / (1.0 - zval))
    curve = barrier_weight * (1.0 / (zval * zval) + 1.0 / ((1.0 - zval) * (1.0 - zval)))
    own_terms = curve * own_vec[param][:1] - slope

    def drain(step, carry):
        to_core(step).wait_send()
        to_chip(step).wait_send()
        scale_to_chip(step).wait_send()
        by, chunk = place(step)

        @pl.when(jnp.logical_not(jnp.logical_and(by == 0, chunk == param)))
        def _():
            message(step, 0, by, chunk).wait_send()

        return carry

    lax.fori_loop(0, STEPS, drain, 0)
    for part in range(2):
        @pl.when(2 * core + part != param)
        def _():
            message(STEPS + part, 0, 0, param).wait_send()

    for piece in range(PIECES):
        to_two_before(piece).wait_send()
        to_pair(piece, landing(2, piece)).wait_send()

    for source in range(4):
        @pl.when(source != param)
        def _():
            message(0, source, 0, param).wait_recv()

        message(0, 4 + source, 1, param).wait_recv()
        message(0, 8 + source, 2, param).wait_recv()
    for high in range(2):
        @pl.when(2 * high + param // 2 != param)
        def _():
            message(0, 12 + high, 0, param).wait_recv()

    out[...] = jnp.sum(m_recv[...], axis=0)[:1] + own_terms


def body(candidate_rows, sigma_rows, sigma_sq_rows, direction, relaxed):
    width, depth = candidate_rows.shape
    f32, bf16 = jnp.float32, jnp.bfloat16
    dma = pltpu.SemaphoreType.DMA
    result = pl.pallas_call(
        kernel,
        out_shape=jax.ShapeDtypeStruct((1, ROWS), f32),
        in_specs=[pl.BlockSpec(memory_space=pl.ANY)] * 3
        + [pl.BlockSpec(memory_space=pltpu.VMEM)] * 2,
        out_specs=pl.BlockSpec(memory_space=pltpu.VMEM),
        scratch_shapes=[
            pltpu.VMEM((3, width, depth), bf16),
            pltpu.VMEM((2, width, depth), bf16),
            pltpu.VMEM((2, depth, width), bf16),
            pltpu.VMEM((4, 8, ROWS), f32),
            pltpu.VMEM((2, 4, 8, ROWS), f32),
            pltpu.VMEM((STEPS, ROWS, width), f32),
            pltpu.VMEM((STEPS, ROWS, width), f32),
            pltpu.VMEM((STEPS, ROWS, width), f32),
            pltpu.VMEM((STEPS, ROWS, HALF), bf16),
            pltpu.VMEM((STEPS, ROWS, HALF), bf16),
            pltpu.VMEM((STEPS, 1, HALF), f32),
            pltpu.VMEM((STEPS, 1, HALF), f32),
            pltpu.VMEM((8, HALF), f32),
            pltpu.VMEM((STEPS + 2, 8, ROWS), f32),
            pltpu.VMEM((14, 8, ROWS), f32),
            dma((5,)),
            dma((PIECES,)), dma((PIECES,)), dma((PIECES,)), dma((PIECES,)),
            dma((STEPS,)), dma((STEPS,)), dma((STEPS,)), dma((STEPS,)), dma((STEPS,)), dma((STEPS,)),
            dma((STEPS + 2,)), dma((14,)), dma((2,)), dma((2,)),
        ],
        compiler_params=pltpu.CompilerParams(
            collective_id=1, has_side_effects=True, vmem_limit_bytes=62 * 2**20
        ),
        name="newton_residual",
    )(
        candidate_rows, sigma_rows, sigma_sq_rows,
        direction.reshape(4, ROWS), relaxed.reshape(1, ROWS),
    )
    return result.reshape(ROWS)


def solution(mesh):
    return jax.shard_map(
        body,
        mesh=mesh,
        in_specs=(
            P("cand", "param"),
            P("cand", "param"),
            P("cand", "param"),
            P("cand"),
            P(("cand", "param")),
        ),
        out_specs=P(("cand", "param")),
        check_vma=False,
    )
```

time: 148 us -> 92 us (0.62)
  Pallas kernels: 142 us -> 90.7 us
  local copies, waits for them, and re-layouts: 4.78 us -> 1.19 us
    pallas_call x1, Pallas kernels: 142 us -> 90.7 us  [body(): pl.pallas_call(kernel, out_shape=jax.ShapeDtypeStruct((1, ROWS), f32), in...]
    unnamed x8 -> x1, local copies, waits for them, and re-layouts: 4.78 us -> 1.19 us
where the time goes in v3:
time: 92 us; the launch traced here: 91.9 us
  Pallas kernels  90.7 us (99%)
  local copies, waits for them, and re-layouts  1.19 us (1%)
    pallas_call x1, Pallas kernels, body(): pl.pallas_call(kernel, out_shape=jax.ShapeDtypeStruct((1, ROWS), f32), in...  90.7 us

profile of v3, /device:TPU:5, one launch (start us, length us, event | category | flops | bytes accessed | tf_op | source)
XLA Modules:
  0.0 91.9 jit_solution(1820556422950145284)
XLA Ops:
  0.0 90.7 %newton_residual.1 = f32[1,128]{1,0:T(1,128)} custom-call(bf16[512,2048]{1,0:T(8,128)(2,1)} %a_in.1, bf16[512,2048]{1,0:T(8,128)(2,1)} %s_in.1, bf16[512,2048]{1,0:T(8,128)(2,1)} %q_in.1, bf16[4,128]{1,0:T(4,128)(2,1)} %bitcast.3, f32[1,128]{1,0:T(1,128)} %bitcast.4), custom_call_target="tpu_custom_call" | custom-call | tf_op jit(solution)/shard_map/newton_residual/pallas_call | solution.py:337
  90.8 1.2 %copy.7 = f32[128]{0:T(128)} copy(f32[128]{0:T(128)} %bitcast.5) | data formatting | bytes 1024

commit v4 on v3

--- a/solution.py
+++ b/solution.py
@@ -12,6 +12,7 @@
 ROWS = 128
 CHUNKS = 4
 STEPS = 3 * CHUNKS
+WHOLE = STEPS - 1
 PIECE = 64
 PIECES = 8
 HALF = 256
@@ -41,7 +42,7 @@
 
 
 def kernel(
-    a_in, s_in, q_in, v_in, z_in, out,
+    a_in, s_in, q_in, v_in, z_in, out, own,
     rows, sq, sqt, own_vec, vec, g_send, g_recv, g_own, k_send, k_recv, w_send, w_recv, col, m_send, m_recv,
     load_sem, z_send_sem, z_recv_sem, x_send_sem, x_recv_sem, g_send_sem, g_recv_sem,
     k_send_sem, k_recv_sem, w_send_sem, w_recv_sem, m_send_sem, m_recv_sem, v_send_sem, v_recv_sem,
@@ -148,24 +149,32 @@
         by = jnp.where(step < CHUNKS, 0, 2 - lax.rem(late, 2))
         return by, jnp.where(step < CHUNKS, step, late // 2)
 
-    def to_core(step):
-        return pltpu.make_async_remote_copy(
-            src_ref=g_send.at[step], dst_ref=g_recv.at[step],
-            send_sem=g_send_sem.at[step], recv_sem=g_recv_sem.at[step],
+    def lines(step, half):
+        if half is None:
+            return step, pl.ds(0, ROWS), step
+        return WHOLE, pl.ds(half * PIECE, PIECE), WHOLE + half
+
+    def to_core(step, half=None):
+        slot, part, turn = lines(step, half)
+        return pltpu.make_async_remote_copy(
+            src_ref=g_send.at[slot, part], dst_ref=g_recv.at[slot, part],
+            send_sem=g_send_sem.at[turn], recv_sem=g_recv_sem.at[turn],
             device_id=(cand, param + 1 - 2 * core), device_id_type=MESH,
         )
 
-    def to_chip(step):
-        return pltpu.make_async_remote_copy(
-            src_ref=k_send.at[step], dst_ref=k_recv.at[step],
-            send_sem=k_send_sem.at[step], recv_sem=k_recv_sem.at[step],
+    def to_chip(step, half=None):
+        slot, part, turn = lines(step, half)
+        return pltpu.make_async_remote_copy(
+            src_ref=k_send.at[slot, part], dst_ref=k_recv.at[slot, part],
+            send_sem=k_send_sem.at[turn], recv_sem=k_recv_sem.at[turn],
             device_id=(cand, lax.rem(param + 2, 4)), device_id_type=MESH,
         )
 
-    def scale_to_chip(step):
-        return pltpu.make_async_remote_copy(
-            src_ref=w_send.at[step], dst_ref=w_recv.at[step],
-            send_sem=w_send_sem.at[step], recv_sem=w_recv_sem.at[step],
+    def scale_to_chip(step, half=None):
+        turn = lines(step, half)[2]
+        return pltpu.make_async_remote_copy(
+            src_ref=w_send.at[turn], dst_ref=w_recv.at[turn],
+            send_sem=w_send_sem.at[turn], recv_sem=w_recv_sem.at[turn],
             device_id=(cand, lax.rem(param + 2, 4)), device_id_type=MESH,
         )
 
@@ -188,7 +197,7 @@
         def _():
             pass_on(0)
 
-        @pl.when(jnp.logical_and(step >= CHUNKS, step < STEPS - 1))
+        @pl.when(step >= CHUNKS)
         def _():
             pass_on(step - CHUNKS + 1)
 
@@ -197,31 +206,44 @@
             for part in range(2):
                 to_pair(2 * chunk + part, landing(2, 2 * chunk + part)).wait_recv()
 
-        left = rows[by, pl.ds(pl.multiple_of(chunk * ROWS, ROWS), ROWS), :]
-        g_send[step] = lax.dot_general(
+        multiply(rows[by, pl.ds(pl.multiple_of(chunk * ROWS, ROWS), ROWS), :], step, None)
+
+    def last_products(half):
+        piece = PIECES - 2 + half
+        to_pair(piece, landing(2, piece)).wait_recv()
+        multiply(rows[1, piece * PIECE : (piece + 1) * PIECE, :], WHOLE, half)
+
+    def multiply(left, step, half):
+        slot, part, _ = lines(step, half)
+        g_send[slot, part] = lax.dot_general(
             left, sqt[1 - core], FIRST, preferred_element_type=jnp.float32
         )
-        to_core(step).start()
-        g_own[step] = lax.dot_general(
+        to_core(step, half).start()
+        g_own[slot, part] = lax.dot_general(
             left, sqt[core], FIRST, preferred_element_type=jnp.float32
         )
 
-    def between_cores(step):
-        to_core(step).wait_recv()
-        total = g_own[step] + g_recv[step]
-        g_own[step] = total
+    def between_cores(step, half=None):
+        slot, part, turn = lines(step, half)
+        to_core(step, half).wait_recv()
+        total = g_own[slot, part] + g_recv[slot, part]
+        g_own[slot, part] = total
         code, scale = coded(total[:, HALF:])
-        k_send[step] = code.astype(jnp.bfloat16)
-        w_send[step] = scale
-        to_chip(step).start()
-        scale_to_chip(step).start()
-
-    def between_chips(step):
+        k_send[slot, part] = code.astype(jnp.bfloat16)
+        w_send[turn] = scale
+        to_chip(step, half).start()
+        scale_to_chip(step, half).start()
+
+    def between_chips(step, halves=(None,)):
         by, chunk = place(step)
-        to_chip(step).wait_recv()
+        other = []
+        for half in halves:
+            slot, part, turn = lines(step, half)
+            to_chip(step, half).wait_recv()
+            scale_to_chip(step, half).wait_recv()
+            other.append(decoded(k_recv[slot, part].astype(jnp.float32), w_recv[turn]))
+        other = jnp.concatenate(other, axis=0) if len(other) > 1 else other[0]
         total = g_own[step]
-        scale_to_chip(step).wait_recv()
-        other = decoded(k_recv[step].astype(jnp.float32), w_recv[step])
         tile = total[:, :HALF] * (total[:, HALF:] + other)
         half_vec = jnp.concatenate([own_vec[2 * core], own_vec[2 * core + 1]], axis=1)
         m_send[step] = exact_dot(2.0 * half_vec, tile, LAST)
@@ -255,6 +277,8 @@
 
         return carry
 
+    wait = jnp.where(odd == 0, 3, 1)
+
     def later(step, carry):
         products(step)
 
@@ -262,6 +286,13 @@
         def _():
             between_chips(step - LAG)
 
+        @pl.when(step >= CHUNKS + wait)
+        def _():
+            between_cores(step - wait)
+
+        return carry
+
+    def left_over(step, carry):
         between_cores(step)
         return carry
 
@@ -273,47 +304,66 @@
     between_cores(CHUNKS - 1)
     for by in (1, 2):
         vec_to(by).wait()
-    lax.fori_loop(CHUNKS, STEPS, later, 0)
-    lax.fori_loop(STEPS - LAG, STEPS, last, 0)
-
-    for part in range(2):
-        m_send[STEPS + part] = col[:, part * ROWS : (part + 1) * ROWS]
-        target = 2 * core + part
-
-        @pl.when(target == param)
-        def _():
-            m_recv[12 + x_hi] = m_send[STEPS + part]
-
-        @pl.when(target != param)
-        def _():
-            message(STEPS + part, 12 + x_hi, 0, target).start()
+    lax.fori_loop(CHUNKS, WHOLE, later, 0)
+    lax.fori_loop(WHOLE - wait, WHOLE - 1, left_over, 0)
+    last_products(0)
+    between_chips(WHOLE - LAG)
+    between_cores(WHOLE - 1)
+    between_cores(WHOLE, 0)
+    last_products(1)
+    between_chips(WHOLE - LAG + 1)
+    between_cores(WHOLE, 1)
+    lax.fori_loop(WHOLE - LAG + 2, WHOLE, last, 0)
 
     zval = z_in[...]
     slope = barrier_weight * (1.0 / zval - 1.0 / (1.0 - zval))
     curve = barrier_weight * (1.0 / (zval * zval) + 1.0 / ((1.0 - zval) * (1.0 - zval)))
-    own_terms = curve * own_vec[param][:1] - slope
+    own[...] = curve * own_vec[param][:1] - slope
 
     def drain(step, carry):
         to_core(step).wait_send()
         to_chip(step).wait_send()
         scale_to_chip(step).wait_send()
-        by, chunk = place(step)
-
-        @pl.when(jnp.logical_not(jnp.logical_and(by == 0, chunk == param)))
-        def _():
-            message(step, 0, by, chunk).wait_send()
-
-        return carry
-
-    lax.fori_loop(0, STEPS, drain, 0)
-    for part in range(2):
-        @pl.when(2 * core + part != param)
-        def _():
-            message(STEPS + part, 0, 0, param).wait_send()
-
+        return carry
+
+    lax.fori_loop(0, WHOLE, drain, 0)
     for piece in range(PIECES):
         to_two_before(piece).wait_send()
         to_pair(piece, landing(2, piece)).wait_send()
+
+    between_chips(WHOLE, (0, 1))
+
+    for part in range(2):
+        m_send[STEPS + part] = col[:, part * ROWS : (part + 1) * ROWS]
+        target = 2 * core + part
+
+        @pl.when(target == param)
+        def _():
+            m_recv[12 + x_hi] = m_send[STEPS + part]
+
+        @pl.when(target != param)
+        def _():
+            message(STEPS + part, 12 + x_hi, 0, target).start()
+
+    for half in range(2):
+        to_core(WHOLE, half).wait_send()
+        to_chip(WHOLE, half).wait_send()
+        scale_to_chip(WHOLE, half).wait_send()
+
+    def sent(step, carry):
+        by, chunk = place(step)
+
+        @pl.when(jnp.logical_not(jnp.logical_and(by == 0, chunk == param)))
+        def _():
+            message(step, 0, by, chunk).wait_send()
+
+        return carry
+
+    lax.fori_loop(0, STEPS, sent, 0)
+    for part in range(2):
+        @pl.when(2 * core + part != param)
+        def _():
+            message(STEPS + part, 0, 0, param).wait_send()
 
     for source in range(4):
         @pl.when(source != param)
@@ -327,19 +377,19 @@
         def _():
             message(0, 12 + high, 0, param).wait_recv()
 
-    out[...] = jnp.sum(m_recv[...], axis=0)[:1] + own_terms
+    out[...] = jnp.sum(m_recv[...], axis=0)[:1]
 
 
 def body(candidate_rows, sigma_rows, sigma_sq_rows, direction, relaxed):
     width, depth = candidate_rows.shape
     f32, bf16 = jnp.float32, jnp.bfloat16
     dma = pltpu.SemaphoreType.DMA
-    result = pl.pallas_call(
+    product, own_terms = pl.pallas_call(
         kernel,
-        out_shape=jax.ShapeDtypeStruct((1, ROWS), f32),
+        out_shape=[jax.ShapeDtypeStruct((1, ROWS), f32)] * 2,
         in_specs=[pl.BlockSpec(memory_space=pl.ANY)] * 3
         + [pl.BlockSpec(memory_space=pltpu.VMEM)] * 2,
-        out_specs=pl.BlockSpec(memory_space=pltpu.VMEM),
+        out_specs=[pl.BlockSpec(memory_space=pltpu.VMEM)] * 2,
         scratch_shapes=[
             pltpu.VMEM((3, width, depth), bf16),
             pltpu.VMEM((2, width, depth), bf16),
@@ -351,14 +401,15 @@
             pltpu.VMEM((STEPS, ROWS, width), f32),
             pltpu.VMEM((STEPS, ROWS, HALF), bf16),
             pltpu.VMEM((STEPS, ROWS, HALF), bf16),
-            pltpu.VMEM((STEPS, 1, HALF), f32),
-            pltpu.VMEM((STEPS, 1, HALF), f32),
+            pltpu.VMEM((STEPS + 1, 1, HALF), f32),
+            pltpu.VMEM((STEPS + 1, 1, HALF), f32),
             pltpu.VMEM((8, HALF), f32),
             pltpu.VMEM((STEPS + 2, 8, ROWS), f32),
             pltpu.VMEM((14, 8, ROWS), f32),
             dma((5,)),
             dma((PIECES,)), dma((PIECES,)), dma((PIECES,)), dma((PIECES,)),
-            dma((STEPS,)), dma((STEPS,)), dma((STEPS,)), dma((STEPS,)), dma((STEPS,)), dma((STEPS,)),
+            dma((STEPS + 1,)), dma((STEPS + 1,)), dma((STEPS + 1,)),
+            dma((STEPS + 1,)), dma((STEPS + 1,)), dma((STEPS + 1,)),
             dma((STEPS + 2,)), dma((14,)), dma((2,)), dma((2,)),
         ],
         compiler_params=pltpu.CompilerParams(
@@ -369,7 +420,7 @@
         candidate_rows, sigma_rows, sigma_sq_rows,
         direction.reshape(4, ROWS), relaxed.reshape(1, ROWS),
     )
-    return result.reshape(ROWS)
+    return (product + own_terms).reshape(ROWS)
 
 
 def solution(mesh):

time: 92 us -> 88.6 us (0.963)
  Pallas kernels: 90.7 us -> 87.3 us
  local copies, waits for them, and re-layouts: 1.19 us -> 0 us
  other arithmetic: 0 us -> 1.15 us
    pallas_call x1, Pallas kernels: 90.7 us -> 87.3 us  [body(): pl.pallas_call(kernel, out_shape=[jax.ShapeDtypeStruct((1, ROWS), f32)] *...]
    unnamed x1 -> x0, local copies, waits for them, and re-layouts: 1.19 us -> none
    reshape x0 -> x1, other arithmetic: none -> 1.15 us  [body(): return (product + own_terms).reshape(ROWS)]
where the time goes in v4:
time: 88.6 us; the launch traced here: 88.4 us
  Pallas kernels  87.3 us (99%)
  other arithmetic  1.15 us (1%)
    pallas_call x1, Pallas kernels, body(): pl.pallas_call(kernel, out_shape=[jax.ShapeDtypeStruct((1, ROWS), f32)] *...  87.3 us

profile of v4, /device:TPU:5, one launch (start us, length us, event | category | flops | bytes accessed | tf_op | source)
XLA Modules:
  0.0 88.4 jit_solution(7405578919375124755)
XLA Ops:
  0.0 87.3 %newton_residual.1 = (f32[1,128]{1,0:T(1,128)}, f32[1,128]{1,0:T(1,128)}) custom-call(bf16[512,2048]{1,0:T(8,128)(2,1)} %a_in.1, bf16[512,2048]{1,0:T(8,128)(2,1)} %s_in.1, bf16[512,2048]{1,0:T(8,128)(2,1)} %q_in.1, bf16[4,128]{1,0:T(4,128)(2,1)} %bitcast.4, f32[1,128]{1,0:T(1,128)} %bitcast.5), custom_call_target="tpu_custom_call" | custom-call | tf_op jit(solution)/shard_map/newton_residual/pallas_call | solution.py:387
  87.3 1.1 %add_bitcast_fusion = f32[128]{0:T(128)} fusion(f32[1,128]{1,0:T(1,128)} %get-tuple-element.7, f32[1,128]{1,0:T(1,128)} %get-tuple-element.8), kind=kLoop, calls=%fused_computation | loop fusion | flops 128 | bytes 1536 | tf_op jit(solution)/shard_map/reshape | solution.py:423

commit v5 on v4

--- a/solution.py
+++ b/solution.py
@@ -18,7 +18,8 @@
 HALF = 256
 SPAN = 256
 AHEAD = 2
-LAG = 4
+DETOUR = range(7, 9)
+LAG = 5
 REACH = 125.0
 LAST = (((1,), (1,)), ((), ()))
 FIRST = (((1,), (0,)), ((), ()))
@@ -43,9 +44,9 @@
 
 def kernel(
     a_in, s_in, q_in, v_in, z_in, out, own,
-    rows, sq, sqt, own_vec, vec, g_send, g_recv, g_own, k_send, k_recv, w_send, w_recv, col, m_send, m_recv,
+    rows, sq, sqt, own_vec, vec, g_send, g_recv, g_own, k_send, k_recv, w_send, w_recv, relay, col, m_send, m_recv,
     load_sem, z_send_sem, z_recv_sem, x_send_sem, x_recv_sem, g_send_sem, g_recv_sem,
-    k_send_sem, k_recv_sem, w_send_sem, w_recv_sem, m_send_sem, m_recv_sem, v_send_sem, v_recv_sem,
+    k_send_sem, k_recv_sem, w_send_sem, w_recv_sem, r_send_sem, r_recv_sem, m_send_sem, m_recv_sem, v_send_sem, v_recv_sem,
 ):
     cand, param = lax.axis_index("cand"), lax.axis_index("param")
     blocks = lax.axis_size("cand")
@@ -170,6 +171,34 @@
             device_id=(cand, lax.rem(param + 2, 4)), device_id_type=MESH,
         )
 
+    def by_odd(step):
+        inside = jnp.logical_and(step >= DETOUR.start, step < DETOUR.stop)
+        return jnp.logical_and(odd == 0, inside)
+
+    def to_relay(step):
+        index = step - DETOUR.start
+        return pltpu.make_async_remote_copy(
+            src_ref=k_send.at[step], dst_ref=relay.at[index],
+            send_sem=k_send_sem.at[step], recv_sem=r_recv_sem.at[index],
+            device_id=(block_at(1), lax.rem(param + 2, 4)), device_id_type=MESH,
+        )
+
+    def from_relay(step):
+        index = step - DETOUR.start
+        return pltpu.make_async_remote_copy(
+            src_ref=relay.at[index], dst_ref=k_recv.at[step],
+            send_sem=r_send_sem.at[index], recv_sem=k_recv_sem.at[step],
+            device_id=(block_at(-1), param), device_id_type=MESH,
+        )
+
+    def hand_back(step):
+        inside = jnp.logical_and(step >= DETOUR.start, step < DETOUR.stop)
+
+        @pl.when(jnp.logical_and(odd == 1, inside))
+        def _():
+            to_relay(step).wait_recv()
+            from_relay(step).start()
+
     def scale_to_chip(step, half=None):
         turn = lines(step, half)[2]
         return pltpu.make_async_remote_copy(
@@ -231,7 +260,16 @@
         code, scale = coded(total[:, HALF:])
         k_send[slot, part] = code.astype(jnp.bfloat16)
         w_send[turn] = scale
-        to_chip(step, half).start()
+        if half is None:
+            @pl.when(by_odd(step))
+            def _():
+                to_relay(step).start()
+
+            @pl.when(jnp.logical_not(by_odd(step)))
+            def _():
+                to_chip(step).start()
+        else:
+            to_chip(step, half).start()
         scale_to_chip(step, half).start()
 
     def between_chips(step, halves=(None,)):
@@ -277,9 +315,10 @@
 
         return carry
 
-    wait = jnp.where(odd == 0, 3, 1)
+    wait = jnp.where(odd == 0, 1, 1)
 
     def later(step, carry):
+        hand_back(step - 2)
         products(step)
 
         @pl.when(step >= LAG)
@@ -327,6 +366,12 @@
         return carry
 
     lax.fori_loop(0, WHOLE, drain, 0)
+
+    @pl.when(odd == 1)
+    def _():
+        for step in DETOUR:
+            from_relay(step).wait_send()
+
     for piece in range(PIECES):
         to_two_before(piece).wait_send()
         to_pair(piece, landing(2, piece)).wait_send()
@@ -403,6 +448,7 @@
             pltpu.VMEM((STEPS, ROWS, HALF), bf16),
             pltpu.VMEM((STEPS + 1, 1, HALF), f32),
             pltpu.VMEM((STEPS + 1, 1, HALF), f32),
+            pltpu.VMEM((len(DETOUR), ROWS, HALF), bf16),
             pltpu.VMEM((8, HALF), f32),
             pltpu.VMEM((STEPS + 2, 8, ROWS), f32),
             pltpu.VMEM((14, 8, ROWS), f32),
@@ -410,6 +456,7 @@
             dma((PIECES,)), dma((PIECES,)), dma((PIECES,)), dma((PIECES,)),
             dma((STEPS + 1,)), dma((STEPS + 1,)), dma((STEPS + 1,)),
             dma((STEPS + 1,)), dma((STEPS + 1,)), dma((STEPS + 1,)),
+            dma((len(DETOUR),)), dma((len(DETOUR),)),
             dma((STEPS + 2,)), dma((14,)), dma((2,)), dma((2,)),
         ],
         compiler_params=pltpu.CompilerParams(

time: 88.6 us -> 86.8 us (0.980)
  Pallas kernels: 87.3 us -> 85.5 us
    pallas_call x1, Pallas kernels: 87.3 us -> 85.5 us  [body(): pl.pallas_call(kernel, out_shape=[jax.ShapeDtypeStruct((1, ROWS), f32)] *...]
where the time goes in v5:
time: 86.8 us; the launch traced here: 86.7 us
  Pallas kernels  85.5 us (99%)
  other arithmetic  1.15 us (1%)
    pallas_call x1, Pallas kernels, body(): pl.pallas_call(kernel, out_shape=[jax.ShapeDtypeStruct((1, ROWS), f32)] *...  85.5 us

profile of v5, /device:TPU:5, one launch (start us, length us, event | category | flops | bytes accessed | tf_op | source)
XLA Modules:
  0.0 86.7 jit_solution(3988561719405232223)
XLA Ops:
  0.0 85.5 %newton_residual.1 = (f32[1,128]{1,0:T(1,128)}, f32[1,128]{1,0:T(1,128)}) custom-call(bf16[512,2048]{1,0:T(8,128)(2,1)} %a_in.1, bf16[512,2048]{1,0:T(8,128)(2,1)} %s_in.1, bf16[512,2048]{1,0:T(8,128)(2,1)} %q_in.1, bf16[4,128]{1,0:T(4,128)(2,1)} %bitcast.4, f32[1,128]{1,0:T(1,128)} %bitcast.5), custom_call_target="tpu_custom_call" | custom-call | tf_op jit(solution)/shard_map/newton_residual/pallas_call | solution.py:432
  85.5 1.1 %add_bitcast_fusion = f32[128]{0:T(128)} fusion(f32[1,128]{1,0:T(1,128)} %get-tuple-element.7, f32[1,128]{1,0:T(1,128)} %get-tuple-element.8), kind=kLoop, calls=%fused_computation | loop fusion | flops 128 | bytes 1536 | tf_op jit(solution)/shard_map/reshape | solution.py:470

commit v6 on v5

--- a/solution.py
+++ b/solution.py
@@ -344,10 +344,9 @@
     for by in (1, 2):
         vec_to(by).wait()
     lax.fori_loop(CHUNKS, WHOLE, later, 0)
-    lax.fori_loop(WHOLE - wait, WHOLE - 1, left_over, 0)
+    lax.fori_loop(WHOLE - wait, WHOLE, left_over, 0)
     last_products(0)
     between_chips(WHOLE - LAG)
-    between_cores(WHOLE - 1)
     between_cores(WHOLE, 0)
     last_products(1)
     between_chips(WHOLE - LAG + 1)

time: 86.8 us -> 86.8 us (level)
  no operation moved by 1% of the time
where the time goes in v6:
time: 86.8 us; the launch traced here: 86.7 us
  Pallas kernels  85.5 us (99%)
  other arithmetic  1.15 us (1%)
    pallas_call x1, Pallas kernels, body(): pl.pallas_call(kernel, out_shape=[jax.ShapeDtypeStruct((1, ROWS), f32)] *...  85.5 us

profile of v6, /device:TPU:5, one launch (start us, length us, event | category | flops | bytes accessed | tf_op | source)
XLA Modules:
  0.0 86.7 jit_solution(4063346432777093069)
XLA Ops:
  0.0 85.5 %newton_residual.1 = (f32[1,128]{1,0:T(1,128)}, f32[1,128]{1,0:T(1,128)}) custom-call(bf16[512,2048]{1,0:T(8,128)(2,1)} %a_in.1, bf16[512,2048]{1,0:T(8,128)(2,1)} %s_in.1, bf16[512,2048]{1,0:T(8,128)(2,1)} %q_in.1, bf16[4,128]{1,0:T(4,128)(2,1)} %bitcast.4, f32[1,128]{1,0:T(1,128)} %bitcast.5), custom_call_target="tpu_custom_call" | custom-call | tf_op jit(solution)/shard_map/newton_residual/pallas_call | solution.py:431
  85.5 1.1 %add_bitcast_fusion = f32[128]{0:T(128)} fusion(f32[1,128]{1,0:T(1,128)} %get-tuple-element.7, f32[1,128]{1,0:T(1,128)} %get-tuple-element.8), kind=kLoop, calls=%fused_computation | loop fusion | flops 128 | bytes 1536 | tf_op jit(solution)/shard_map/reshape | solution.py:469
